TPU v7x, 32 devices: a whole 2x2x4 slice. The times are simulated.
32 devices in a mesh: row: 2 (over x), col: 4 (over y, core), depth: 4 (over z).
Axes of the slice: x: 2, y: 2, z: 4, core: 2. Of those that a mesh axis runs over, the one named last changes fastest.
Arguments:
- activations: float32 [256, 8192], P(('col', 'depth'), 'row'), may hold values from -0.375 to 0.375
- grad_output: float32 [256, 16384], P('row', ('col', 'depth')), may hold values from -6 to 6
- up_weight: float32 [8192, 16384], P('row', ('col', 'depth')), may hold values from -0.0625 to 0.0625
Outputs:
- grad_input: float32 [256, 8192], P(('col', 'depth'), 'row')
- grad_weight: float32 [8192, 16384], P('row', ('col', 'depth'))
All inputs are finite; a program needn't handle non-finite values.
Results may differ from a plain program's by a relative error of at most 0.000075.
Values sent between devices are 32-bit elements; how exact they have to be, the bound alone decides.
A program may use at most 128 MiB of HBM per device.

v0:
```python
import jax
import jax.numpy as jnp
from jax import lax
from jax.sharding import PartitionSpec as P


def shards(activations, grad_output, up_weight):
    highest = lax.Precision.HIGHEST
    all_feats = lax.all_gather(activations, ("col", "depth"), axis=0, tiled=True)
    all_grads = lax.all_gather(grad_output, "row", axis=0, tiled=True)
    part_input = jnp.dot(
        all_grads, up_weight.T, precision=highest, preferred_element_type=jnp.float32
    )
    grad_weight = jnp.dot(
        all_feats.T, all_grads, precision=highest, preferred_element_type=jnp.float32
    )
    by_column = lax.psum_scatter(part_input, "col", scatter_dimension=0, tiled=True)
    grad_input = lax.psum_scatter(by_column, "depth", scatter_dimension=0, tiled=True)
    return (grad_input, grad_weight)


def solution(mesh):
    return jax.shard_map(
        shards,
        mesh=mesh,
        in_specs=(
            P(("col", "depth"), "row"),
            P("row", ("col", "depth")),
            P("row", ("col", "depth")),
        ),
        out_specs=(P(("col", "depth"), "row"), P("row", ("col", "depth"))),
        check_vma=False,
    )
```

profile of v0, /device:TPU:17, one launch (start us, length us, event | category | flops | bytes accessed | tf_op | source)
XLA Modules:
  0.0 146.0 jit_solution(13598712250296703620)
XLA Ops:
  8.0 0.0 all-gather.3.cloned.1.call-start
  8.0 0.7 all-gather.3.cloned.1.call-update
  8.7 0.0 reduce-scatter.3.cloned.1.call-start
  8.8 24.0 %all-gather.3.cloned.1.call-done = f32[256,1024]{1,0:T(8,128)} async-done(((f32[128,1024]{1,0:T(8,128)}), f32[256,1024]{1,0:T(8,128)}) %all-gather.3.cloned.1.call-update) | async-done | bytes 1048592 | tf_op jit(solution)/shard_map/all_gather | solution.py:10
  32.8 0.0 copy-start
  32.8 19.3 %fusion = f32[256,4096]{1,0:T(8,128)} fusion(f32[256,1024]{1,0:T(8,128)} %all-gather.3.cloned.1.call-done, f32[4096,1024]{1,0:T(8,128)} %param.5), kind=kOutput, calls=%fused_computation | convolution fusion | flops 12884901888 | bytes 22020096 | tf_op jit(solution)/shard_map/dot_general | solution.py:11
  52.1 0.0 reduce-scatter.3.cloned.1.call-update
  52.1 0.0 all-gather.5.cloned.1.call-start
  52.2 0.5 all-gather.5.cloned.1.call-update
  52.7 0.0 reduce-scatter.5.cloned.1.call-start
  52.8 44.1 %reduce-scatter.3.cloned.1.call-done = f32[64,4096]{1,0:T(8,128)} async-done(((f32[256,4096]{1,0:T(8,128)}), f32[64,4096]{1,0:T(8,128)}) %reduce-scatter.3.cloned.1.call-update) | async-done | bytes 1048592 | tf_op jit(solution)/shard_map/reduce_scatter | solution.py:17
  96.9 0.0 reduce-scatter.5.cloned.1.call-update
  96.9 24.7 %all-gather.5.cloned.1.call-done = f32[256,4096]{1,0:T(8,128)} async-done(((f32[16,4096]{1,0:T(8,128)}), f32[256,4096]{1,0:T(8,128)}) %all-gather.5.cloned.1.call-update) | async-done | bytes 4194320 | tf_op jit(solution)/shard_map/all_gather | solution.py:9
  121.6 0.0 copy-done
  121.6 17.2 %fusion.1 = f32[4096,1024]{1,0:T(8,128)} fusion(f32[256,4096]{1,0:T(8,128)} %all-gather.5.cloned.1.call-done, f32[256,1024]{1,0:T(8,128)S(1)} %copy-done), kind=kOutput, calls=%fused_computation.1 | convolution fusion | flops 12884901888 | bytes 22020096 | tf_op jit(solution)/shard_map/dot_general | solution.py:14
  138.9 0.0 reduce-scatter.5.cloned.1.call-done
Async XLA Ops:
  8.0 24.8 %all-gather.3.cloned.1.call-start = ((), (), s32[]{:S(2)}) async-start(), calls=%async_computation.2 | async-start | bytes 1572864 | tf_op jit(solution)/shard_map/all_gather | solution.py:10
  8.7 88.1 %reduce-scatter.3.cloned.1.call-start = ((), (), s32[]{:S(2)}) async-start(), calls=%async_computation.3 | async-start | bytes 5242880 | tf_op jit(solution)/shard_map/reduce_scatter | solution.py:17
  32.8 88.8 %copy-start = (f32[256,1024]{1,0:T(8,128)S(1)}, f32[256,1024]{1,0:T(8,128)}, u32[]{:S(2)}) copy-start(f32[256,1024]{1,0:T(8,128)} %all-gather.3.cloned.1.call-done) | copy-start | bytes 3145732
  52.1 69.5 %all-gather.5.cloned.1.call-start = ((), (), s32[]{:S(2)}) async-start(), calls=%async_computation.5 | async-start | bytes 4456448 | tf_op jit(solution)/shard_map/all_gather | solution.py:9
  52.7 86.1 %reduce-scatter.5.cloned.1.call-start = ((), (), s32[]{:S(2)}) async-start(), calls=%async_computation.4 | async-start | bytes 1310720 | tf_op jit(solution)/shard_map/reduce_scatter | solution.py:18
Sparse Core Ops, SparseCore 0:
  10.4 22.3 all-gather.2
  52.3 44.5 reduce-scatter.2
  99.8 31.8 reduce-scatter.4
Sparse Core Ops, SparseCore 1:
  54.8 66.7 all-gather.4
where the time goes:
time: 149 us; the launch traced here: 146 us
  waiting for transfers between devices  94.1 us (63%)
  matrix products  36.6 us (25%)
  between operations  15.2 us (10%)
    reduce_scatter x1, waiting for transfers between devices, shards(): lax.psum_scatter(part_input, 'col', scatter_dimension=0, tiled=True)  44.1 us
    all_gather x1, waiting for transfers between devices, shards(): lax.all_gather(activations, ('col', 'depth'), axis=0, tiled=True)  24.7 us
    all_gather x1, waiting for transfers between devices, shards(): all_grads = lax.all_gather(grad_output, 'row', axis=0, tiled=True)  24 us
    dot_general x1, matrix products, shards(): jnp.dot(all_grads, up_weight.T, precision=highest, preferred_element_type...  19.3 us
    dot_general x1, matrix products, shards(): jnp.dot(all_feats.T, all_grads, precision=highest, preferred_element_type...  17.2 us
  transfers between devices with their start and end apart: 4, of which 3 were waited for; matrix products, arithmetic and copies ran while one was open for 12% of the time, Pallas kernels for 0%

commit v1 on v0

v1 whole, which is shorter than its diff:
```python
import functools

import jax
import jax.numpy as jnp
from jax import lax
from jax.experimental import pallas as pl
from jax.experimental.pallas import tpu as pltpu
from jax.sharding import PartitionSpec as P

MESH = pl.DeviceIdType.MESH
NY = 2
UP, DOWN, ACROSS, PAIR = range(4)


def both(a, b):
    return jnp.logical_and(a, b)


def split(value):
    high = value.astype(jnp.bfloat16)
    low = (value - high.astype(jnp.float32)).astype(jnp.bfloat16)
    return high, low


def dot_nt(a, b):
    return lax.dot_general(
        a, b, (((1,), (1,)), ((), ())), preferred_element_type=jnp.float32
    )


def exchange_kernel(
    rows, nd, cuts, tile,
    acts_ref, grads_ref, weight_ref,
    out_ref, ath_ref, atl_ref, gh_ref, gl_ref,
    acts, grads, stage, wh, wl, part, rc, ry_a, ry_b, rz_a, rz_b,
    w_sem, x_s, x_r, ag_s, ag_r, c_s, c_r, ya_s, ya_r, yb_s, yb_r, za_s, za_r, zb_s, zb_r,
):
    x = lax.axis_index("row")
    col = lax.axis_index("col")
    z = lax.axis_index("depth")
    y, c = col // 2, col % 2
    oy, oc = 1 - y, 1 - c
    y1 = x * NY // rows
    tb, dm = acts_ref.shape
    trow = grads_ref.shape[0]
    tiles = dm // tile
    per = rows // NY
    has_up, has_down = z < nd - 1, z > 0

    mate = {"col": 2 * y + oc}
    across = {"col": 2 * oy + c}
    above, below = {"depth": z + 1}, {"depth": z - 1}

    def blk(yy, cc, zz):
        return (2 * yy + cc) * nd + zz

    me = blk(y, c, z)
    started = []

    def send(cond, make):
        def go():
            make().start()

        started.append((cond, make))
        if cond is None:
            go()
        else:
            pl.when(cond)(go)

    def weight_copy(i, slot):
        return pltpu.make_async_copy(
            weight_ref.at[pl.ds(i * tile, tile), :], stage.at[slot], w_sem.at[slot]
        )

    slots = min(3, tiles)
    for i in range(slots):
        weight_copy(i, i).start()

    acts[me] = acts_ref[...]
    grads[x] = grads_ref[...]

    barrier = pltpu.get_barrier_semaphore()
    peers = [{"row": (x + d) % rows} for d in range(1, rows)]
    for peer in [mate, across] + peers:
        pl.semaphore_signal(barrier, inc=1, device_id=peer, device_id_type=MESH)

    @pl.when(has_up)
    def _():
        pl.semaphore_signal(barrier, inc=1, device_id=above, device_id_type=MESH)

    @pl.when(has_down)
    def _():
        pl.semaphore_signal(barrier, inc=1, device_id=below, device_id_type=MESH)

    lines = has_up.astype(jnp.int32) + has_down.astype(jnp.int32)
    pl.semaphore_wait(barrier, 2 + len(peers) + lines)

    def x_copy(d):
        return pltpu.make_async_remote_copy(
            src_ref=grads.at[x], dst_ref=grads.at[x],
            send_sem=x_s.at[d], recv_sem=x_r.at[x],
            device_id={"row": (x + d) % rows}, device_id_type=MESH,
        )

    for d in range(1, rows):
        send(None, functools.partial(x_copy, d))

    targets = {UP: above, DOWN: below, ACROSS: across, PAIR: mate}

    def ag_copy(p, b, way):
        ref = acts.at[b, :, pl.ds(cuts[p], cuts[p + 1] - cuts[p])]
        return pltpu.make_async_remote_copy(
            src_ref=ref, dst_ref=ref,
            send_sem=ag_s.at[p, b, way], recv_sem=ag_r.at[p, b],
            device_id=targets[way], device_id_type=MESH,
        )

    def ag_send(cond, p, b, way):
        send(cond, lambda: ag_copy(p, b, way))

    def ag_wait(cond, p, b):
        def go():
            ag_copy(p, b, PAIR).wait_recv()

        if cond is None:
            go()
        else:
            pl.when(cond)(go)

    for p in range(2):
        ag_send(has_up, p, me, UP)
        ag_send(has_down, p, me, DOWN)
    ag_send(None, 1, me, ACROSS)
    ag_send(None, 0, me, ACROSS)
    for p in range(2):
        ag_send(None, p, me, PAIR)

    def ag_line(p, yy, s):
        low, high = z - s >= 0, z + s <= nd - 1
        b_low, b_high = blk(yy, c, z - s), blk(yy, c, z + s)
        ag_wait(low, p, b_low)
        ag_send(both(low, has_up), p, b_low, UP)
        if p == 0:
            ag_send(low, p, b_low, ACROSS)
        ag_send(low, p, b_low, PAIR)
        ag_wait(high, p, b_high)
        ag_send(both(high, has_down), p, b_high, DOWN)
        if p == 0:
            ag_send(high, p, b_high, ACROSS)
        ag_send(high, p, b_high, PAIR)

    def ag_cross(p, s):
        if s == 0:
            b = blk(oy, c, z)
            ag_wait(None, p, b)
            if p == 1:
                ag_send(has_up, p, b, UP)
                ag_send(has_down, p, b, DOWN)
            ag_send(None, p, b, PAIR)
        elif p == 1:
            ag_line(1, oy, s)
        else:
            for cond, b in (
                (z - s >= 0, blk(oy, c, z - s)),
                (z + s <= nd - 1, blk(oy, c, z + s)),
            ):
                ag_wait(cond, 0, b)
                ag_send(cond, 0, b, PAIR)

    def partial(phase):
        yy = (y1 + phase) % NY
        for j in range(per):
            q = yy * per + j

            @pl.when(q != x)
            def _():
                pltpu.make_async_remote_copy(
                    src_ref=grads.at[q], dst_ref=grads.at[q],
                    send_sem=x_s.at[0], recv_sem=x_r.at[q],
                    device_id=mate, device_id_type=MESH,
                ).wait_recv()

            high, low = split(grads[q])
            at = pl.ds(pl.multiple_of(q * trow, trow), trow)
            gh_ref[at, :] = high
            gl_ref[at, :] = low
        half = per * trow
        at = pl.ds(pl.multiple_of(yy * half, half), half)

        def step(i, carry):
            rows_at = pl.ds(pl.multiple_of(i * tile, tile), tile)
            if phase == 0:
                slot = i % slots
                weight_copy(i, slot).wait()
                high, low = split(stage[slot])
                wh[rows_at, :] = high
                wl[rows_at, :] = low

                @pl.when(i + slots < tiles)
                def _():
                    weight_copy(i + slots, slot).start()
            else:
                high, low = wh[rows_at, :], wl[rows_at, :]
            g_high, g_low = gh_ref[at, :], gl_ref[at, :]
            total = dot_nt(g_high, high) + (dot_nt(g_low, high) + dot_nt(g_high, low))
            part[pl.ds(yy * 2 * nd, 2 * nd), :, rows_at] = total.reshape(
                2 * nd, tb, tile
            )
            return carry

        lax.fori_loop(0, tiles, step, 0)

    def cols(p):
        return pl.ds(cuts[p], cuts[p + 1] - cuts[p])

    def pair_copy(yy, p):
        return pltpu.make_async_remote_copy(
            src_ref=part.at[pl.ds(blk(yy, oc, 0), nd), :, cols(p)],
            dst_ref=rc.at[yy, :, :, cols(p)],
            send_sem=c_s.at[yy, p], recv_sem=c_r.at[yy, p],
            device_id=mate, device_id_type=MESH,
        )

    def pair_send(phase):
        yy = (y1 + phase) % NY
        for p in range(2):
            send(None, functools.partial(pair_copy, yy, p))

    def pair_add(phase, p):
        yy = (y1 + phase) % NY
        pair_copy(yy, p).wait_recv()
        own = pl.ds(blk(yy, c, 0), nd)
        part[own, :, cols(p)] += rc[yy, :, :, cols(p)]

    def across_copy(t):
        return pltpu.make_async_remote_copy(
            src_ref=part.at[blk(oy, c, t), :, cols(0)], dst_ref=ry_a.at[t],
            send_sem=ya_s.at[t], recv_sem=ya_r.at[t],
            device_id=across, device_id_type=MESH,
        )

    def across_send(phase):
        yy = (y1 + phase) % NY
        order = sorted(range(nd), key=lambda t: -abs(2 * t - nd + 1))
        for t in order:
            send(yy != y, functools.partial(across_copy, t))

    def across_add():
        order = sorted(range(nd), key=lambda t: -abs(2 * t - nd + 1))
        for t in order:
            across_copy(t).wait_recv()
            part[blk(y, c, t), :, cols(0)] += ry_a[t]

    def line_copy(p, yy, t, way):
        if p == 0:
            dst, ss, rs = rz_a.at[way, t], za_s.at[way, t], za_r.at[way, t]
        else:
            dst, ss, rs = rz_b.at[yy, way, t], zb_s.at[yy, way, t], zb_r.at[yy, way, t]
        return pltpu.make_async_remote_copy(
            src_ref=part.at[blk(yy, c, t), :, cols(p)], dst_ref=dst,
            send_sem=ss, recv_sem=rs,
            device_id=targets[way], device_id_type=MESH,
        )

    def line_take(p, yy, t, way):
        line_copy(p, yy, t, way).wait_recv()
        got = rz_a[way, t] if p == 0 else rz_b[yy, way, t]
        part[blk(yy, c, t), :, cols(p)] += got

    def line_step(p, yy, s, cond=None):
        for t, way, mine, more in (
            (nd - 1 - s, UP, z < nd - 1 - s, has_down),
            (s, DOWN, z > s, has_up),
        ):
            on = mine if cond is None else both(cond, mine)
            pl.when(both(on, more))(functools.partial(line_take, p, yy, t, way))
            send(on, functools.partial(line_copy, p, yy, t, way))

    def line_end(p, yy, cond=None):
        for way, more in ((UP, has_down), (DOWN, has_up)):
            on = more if cond is None else both(cond, more)
            pl.when(on)(functools.partial(line_take, p, yy, z, way))

    def last_copy():
        return pltpu.make_async_remote_copy(
            src_ref=part.at[blk(oy, c, z), :, cols(1)], dst_ref=ry_b,
            send_sem=yb_s, recv_sem=yb_r,
            device_id=across, device_id_type=MESH,
        )

    y2 = (y1 + 1) % NY
    first, second = y == y1, y != y1

    partial(0)
    pair_send(0)
    ag_cross(1, 0)
    ag_line(0, y, 1)
    ag_line(1, y, 1)
    pair_add(0, 0)
    across_send(0)
    pair_add(0, 1)
    line_step(1, y1, 0)
    ag_cross(0, 0)
    ag_cross(1, 1)
    ag_line(0, y, 2)
    ag_line(1, y, 2)
    partial(1)
    pair_send(1)
    line_step(1, y1, 1)
    pair_add(1, 0)
    across_send(1)
    pair_add(1, 1)
    line_step(1, y2, 0)
    for s in range(3, nd):
        ag_line(0, y, s)
        ag_line(1, y, s)
    for s in range(2, nd):
        ag_cross(1, s)
    pl.when(first)(across_add)
    line_step(0, y, 0, first)
    for s in range(2, nd - 1):
        line_step(1, y1, s)
    line_step(0, y, 1, first)
    line_step(1, y2, 1)
    line_end(1, y1)
    send(second, last_copy)
    pl.when(second)(across_add)
    line_step(0, y, 0, second)
    for s in range(2, nd - 1):
        line_step(0, y, s, first)
    for s in range(2, nd - 1):
        line_step(1, y2, s)
    line_step(0, y, 1, second)
    line_end(1, y2)
    send(first, last_copy)
    for s in range(2, nd - 1):
        line_step(0, y, s, second)

    for s in range(1, nd):
        ag_cross(0, s)
    for p in range(2):
        for yy in range(NY):
            for zz in range(nd):
                ag_wait(None, p, blk(yy, oc, zz))

    def turn(i, carry):
        at = pl.ds(pl.multiple_of(i * tile, tile), tile)
        block = acts[:, :, at].reshape(2 * NY * nd * tb, tile)
        high, low = split(block.T)
        ath_ref[at, :] = high
        atl_ref[at, :] = low
        return carry

    lax.fori_loop(0, tiles, turn, 0)

    line_end(0, y)
    last_copy().wait_recv()
    part[me, :, cols(1)] += ry_b[...]
    out_ref[...] = part[me]

    for cond, make in started:
        if cond is None:
            make().wait_send()
        else:
            pl.when(cond)(lambda make=make: make().wait_send())


def weight_kernel(ath_ref, atl_ref, gh_ref, gl_ref, out_ref):
    def dot(a, b):
        return jnp.dot(a, b, preferred_element_type=jnp.float32)

    high = ath_ref[...]
    out_ref[...] = dot(high, gh_ref[...]) + (
        dot(high, gl_ref[...]) + dot(atl_ref[...], gh_ref[...])
    )


def shards(rows, nc, nd, activations, grad_output, up_weight):
    tb, dm = activations.shape
    trow, df = grad_output.shape
    tokens = trow * rows
    tile = min(512, dm)
    f32, bf16 = jnp.float32, jnp.bfloat16
    step = max(128, dm // 8)
    cuts = (0, (dm // step * 5 // 8) * step, dm)
    wa, wb = cuts[1], dm - cuts[1]
    vmem = pl.BlockSpec(memory_space=pltpu.VMEM)
    dma = pltpu.SemaphoreType.DMA
    grad_input, ath, atl, gh, gl = pl.pallas_call(
        functools.partial(exchange_kernel, rows, nd, cuts, tile),
        out_shape=(
            jax.ShapeDtypeStruct((tb, dm), f32),
            jax.ShapeDtypeStruct((dm, tokens), bf16),
            jax.ShapeDtypeStruct((dm, tokens), bf16),
            jax.ShapeDtypeStruct((tokens, df), bf16),
            jax.ShapeDtypeStruct((tokens, df), bf16),
        ),
        in_specs=[vmem, vmem, pl.BlockSpec(memory_space=pl.ANY)],
        out_specs=(vmem,) * 5,
        scratch_shapes=[
            pltpu.VMEM((nc * nd, tb, dm), f32),
            pltpu.VMEM((rows, trow, df), f32),
            pltpu.VMEM((min(3, dm // tile), tile, df), f32),
            pltpu.VMEM((dm, df), bf16),
            pltpu.VMEM((dm, df), bf16),
            pltpu.VMEM((nc * nd, tb, dm), f32),
            pltpu.VMEM((NY, nd, tb, dm), f32),
            pltpu.VMEM((nd, tb, wa), f32),
            pltpu.VMEM((tb, wb), f32),
            pltpu.VMEM((2, nd, tb, wa), f32),
            pltpu.VMEM((NY, 2, nd, tb, wb), f32),
            dma((3,)),
            dma((rows,)),
            dma((rows,)),
            dma((2, nc * nd, 4)),
            dma((2, nc * nd)),
            dma((NY, 2)),
            dma((NY, 2)),
            dma((nd,)),
            dma((nd,)),
            dma,
            dma,
            dma((2, nd)),
            dma((2, nd)),
            dma((NY, 2, nd)),
            dma((NY, 2, nd)),
        ],
        compiler_params=pltpu.CompilerParams(
            collective_id=0, has_side_effects=True, vmem_limit_bytes=60 * 2**20
        ),
        cost_estimate=pl.CostEstimate(
            flops=6 * tokens * dm * df, bytes_accessed=4 * dm * df, transcendentals=0
        ),
        name="exchange",
    )(activations, grad_output, up_weight)

    grad_weight = pl.pallas_call(
        weight_kernel,
        grid=(dm // tile,),
        out_shape=jax.ShapeDtypeStruct((dm, df), f32),
        in_specs=[
            pl.BlockSpec((tile, tokens), lambda i: (i, 0)),
            pl.BlockSpec((tile, tokens), lambda i: (i, 0)),
            pl.BlockSpec((tokens, df), lambda i: (0, 0)),
            pl.BlockSpec((tokens, df), lambda i: (0, 0)),
        ],
        out_specs=pl.BlockSpec((tile, df), lambda i: (i, 0)),
        compiler_params=pltpu.CompilerParams(vmem_limit_bytes=48 * 2**20),
        cost_estimate=pl.CostEstimate(
            flops=6 * tokens * dm * df, bytes_accessed=4 * dm * df, transcendentals=0
        ),
        name="weight_grad",
    )(ath, atl, gh, gl)
    return grad_input, grad_weight


def solution(mesh):
    rows, nc, nd = (mesh.shape[name] for name in ("row", "col", "depth"))
    return jax.shard_map(
        functools.partial(shards, rows, nc, nd),
        mesh=mesh,
        in_specs=(
            P(("col", "depth"), "row"),
            P("row", ("col", "depth")),
            P("row", ("col", "depth")),
        ),
        out_specs=(P(("col", "depth"), "row"), P("row", ("col", "depth"))),
        check_vma=False,
    )
```

time: 149 us -> 100 us (0.67); the launches traced: 146 us -> 99.4 us
  waiting for transfers between devices: 94.1 us -> 0 us
  Pallas kernels: 0 us -> 92.8 us
  matrix products: 36.6 us -> 0 us
  between operations: 15.2 us -> 0.65 us
  local copies, waits for them, and re-layouts: 0.01 us -> 5.96 us
    pallas_call x0 -> x2, Pallas kernels: none -> 92.8 us  [the longest x1 82.6 us: shards(): pl.pallas_call(functools.partial(exchange_kernel, rows, nd, cuts, tile),...]
    all_gather x2 -> x0, waiting for transfers between devices: 48.7 us -> none  [the longest x1 24.7 us: shards(): lax.all_gather(activations, ('col', 'depth'), axis=0, tiled=True)]
    reduce_scatter x2 -> x0, waiting for transfers between devices: 44.1 us -> none  [the longest x1 44.1 us: shards(): lax.psum_scatter(part_input, 'col', scatter_dimension=0, tiled=True)]
    dot_general x2 -> x0, matrix products: 36.6 us -> none  [the longest x1 19.3 us: shards(): jnp.dot(all_grads, up_weight.T, precision=highest, preferred_element_type...]
    unnamed x2 -> x11, local copies, waits for them, and re-layouts: 0.01 us -> 5.96 us
  transfers between devices with their start and end apart: 4 -> 0, of which waited for: 3 -> 0; matrix products, arithmetic and copies ran while one was open for 12% -> 0% of each run, Pallas kernels for 0% -> 0%
where the time goes in v1:
time: 100 us; the launch traced here: 99.4 us
  Pallas kernels  92.8 us (93%)
  local copies, waits for them, and re-layouts  5.96 us (6%)
    pallas_call x1, Pallas kernels, shards(): pl.pallas_call(functools.partial(exchange_kernel, rows, nd, cuts, tile),...  82.6 us
    pallas_call x1, Pallas kernels, shards(): pl.pallas_call(weight_kernel, grid=(dm // tile,), out_shape=jax.ShapeDtyp...  10.2 us
    unnamed x11, local copies, waits for them, and re-layouts  5.96 us

profile of v1, /device:TPU:17, one launch (start us, length us, event | category | flops | bytes accessed | tf_op | source)
XLA Modules:
  0.0 99.4 jit_solution(12142817657053636574)
XLA Ops:
  0.6 82.6 %exchange.1 = (f32[16,4096]{1,0:T(8,128)}, bf16[4096,256]{1,0:T(8,128)(2,1)}, bf16[4096,256]{1,0:T(8,128)(2,1)}, bf16[256,1024]{1,0:T(8,128)(2,1)}, bf16[256,1024]{1,0:T(8,128)(2,1)}) custom-call(f32[16,4096]{1,0:T(8,128)} %acts_ref.1, f32[128,1024]{1,0:T(8,128)} %grads_ref.1, f32[4096,1024]{1,0:T(8,128)} %weight_ref.1), custom_call_target="tpu_custom_call" | custom-call | flops 6442450944 | bytes 16777216 | tf_op jit(solution)/shard_map/exchange/pallas_call | solution.py:389
  83.2 0.0 copy-start
  83.2 1.6 %copy-done = bf16[4096,256]{1,0:T(8,128)(2,1)S(1)} copy-done((bf16[4096,256]{1,0:T(8,128)(2,1)S(1)}, bf16[4096,256]{1,0:T(8,128)(2,1)}, u32[]{:S(2)}) %copy-start) | copy-done | bytes 2097176
  84.8 0.0 copy-start.1
  84.8 1.6 %copy-done.1 = bf16[4096,256]{1,0:T(8,128)(2,1)S(1)} copy-done((bf16[4096,256]{1,0:T(8,128)(2,1)S(1)}, bf16[4096,256]{1,0:T(8,128)(2,1)}, u32[]{:S(2)}) %copy-start.1) | copy-done | bytes 2097176
  86.4 0.0 copy-start.2
  86.4 1.0 %copy-done.2 = bf16[256,1024]{1,0:T(8,128)(2,1)S(1)} copy-done((bf16[256,1024]{1,0:T(8,128)(2,1)S(1)}, bf16[256,1024]{1,0:T(8,128)(2,1)}, u32[]{:S(2)}) %copy-start.2) | copy-done | bytes 524312
  87.5 0.0 copy-start.3
  87.5 1.0 %copy-done.3 = bf16[256,1024]{1,0:T(8,128)(2,1)S(1)} copy-done((bf16[256,1024]{1,0:T(8,128)(2,1)S(1)}, bf16[256,1024]{1,0:T(8,128)(2,1)}, u32[]{:S(2)}) %copy-start.3) | copy-done | bytes 524312
  88.5 0.0 copy-start.4
  88.5 10.2 %weight_grad.1 = f32[4096,1024]{1,0:T(8,128)} custom-call(bf16[4096,256]{1,0:T(8,128)(2,1)S(1)} %copy-done, bf16[4096,256]{1,0:T(8,128)(2,1)S(1)} %copy-done.1, bf16[256,1024]{1,0:T(8,128)(2,1)S(1)} %copy-done.2, bf16[256,1024]{1,0:T(8,128)(2,1)S(1)} %copy-done.3), custom_call_target="tpu_custom_call" | custom-call | flops 6442450944 | bytes 16777216 | tf_op jit(solution)/shard_map/weight_grad/pallas_call | solution.py:437
  98.7 0.0 copy-done.4
  98.7 0.7 copy.6
Async XLA Ops:
  83.2 1.6 %copy-start = (bf16[4096,256]{1,0:T(8,128)(2,1)S(1)}, bf16[4096,256]{1,0:T(8,128)(2,1)}, u32[]{:S(2)}) copy-start(bf16[4096,256]{1,0:T(8,128)(2,1)} %get-tuple-element.8.ath_ref) | copy-start | bytes 6291460
  84.8 1.6 %copy-start.1 = (bf16[4096,256]{1,0:T(8,128)(2,1)S(1)}, bf16[4096,256]{1,0:T(8,128)(2,1)}, u32[]{:S(2)}) copy-start(bf16[4096,256]{1,0:T(8,128)(2,1)} %get-tuple-element.9.atl_ref) | copy-start | bytes 6291460
  86.4 1.0 %copy-start.2 = (bf16[256,1024]{1,0:T(8,128)(2,1)S(1)}, bf16[256,1024]{1,0:T(8,128)(2,1)}, u32[]{:S(2)}) copy-start(bf16[256,1024]{1,0:T(8,128)(2,1)} %get-tuple-element.10.gh_ref) | copy-start | bytes 1572868
  87.5 1.0 %copy-start.3 = (bf16[256,1024]{1,0:T(8,128)(2,1)S(1)}, bf16[256,1024]{1,0:T(8,128)(2,1)}, u32[]{:S(2)}) copy-start(bf16[256,1024]{1,0:T(8,128)(2,1)} %get-tuple-element.11.gl_ref) | copy-start | bytes 1572868
  88.5 10.2 %copy-start.4 = (f32[16,4096]{1,0:T(8,128)S(1)}, f32[16,4096]{1,0:T(8,128)}, u32[]{:S(2)}) copy-start(f32[16,4096]{1,0:T(8,128)} %get-tuple-element.14) | copy-start | bytes 786436

commit v2 on v1

--- a/solution.py
+++ b/solution.py
@@ -32,8 +32,8 @@
     rows, nd, cuts, tile,
     acts_ref, grads_ref, weight_ref,
     out_ref, ath_ref, atl_ref, gh_ref, gl_ref,
-    acts, grads, stage, wh, wl, part, rc, ry_a, ry_b, rz_a, rz_b,
-    w_sem, x_s, x_r, ag_s, ag_r, c_s, c_r, ya_s, ya_r, yb_s, yb_r, za_s, za_r, zb_s, zb_r,
+    acts, grads, gcat, th, tl, stage, wh, wl, part, rc, ry_a, ry_b, rz_a, rz_b,
+    t_sem, w_sem, x_s, x_r, ag_s, ag_r, c_s, c_r, ya_s, ya_r, yb_s, yb_r, za_s, za_r, zb_s, zb_r,
 ):
     x = lax.axis_index("row")
     col = lax.axis_index("col")
@@ -167,7 +167,9 @@
                 ag_wait(cond, 0, b)
                 ag_send(cond, 0, b, PAIR)
 
-    def partial(phase):
+    half = per * trow
+
+    def prepare(phase):
         yy = (y1 + phase) % NY
         for j in range(per):
             q = yy * per + j
@@ -184,8 +186,11 @@
             at = pl.ds(pl.multiple_of(q * trow, trow), trow)
             gh_ref[at, :] = high
             gl_ref[at, :] = low
-        half = per * trow
-        at = pl.ds(pl.multiple_of(yy * half, half), half)
+            gcat[phase, j * trow : (j + 1) * trow, :] = high
+            gcat[phase, half + j * trow : half + (j + 1) * trow, :] = low
+
+    def partial(phase, p):
+        yy = (y1 + phase) % NY
 
         def step(i, carry):
             rows_at = pl.ds(pl.multiple_of(i * tile, tile), tile)
@@ -201,14 +206,14 @@
                     weight_copy(i + slots, slot).start()
             else:
                 high, low = wh[rows_at, :], wl[rows_at, :]
-            g_high, g_low = gh_ref[at, :], gl_ref[at, :]
-            total = dot_nt(g_high, high) + (dot_nt(g_low, high) + dot_nt(g_high, low))
+            pairs = dot_nt(gcat[phase], high)
+            total = pairs[:half] + (pairs[half:] + dot_nt(gcat[phase, :half, :], low))
             part[pl.ds(yy * 2 * nd, 2 * nd), :, rows_at] = total.reshape(
                 2 * nd, tb, tile
             )
             return carry
 
-        lax.fori_loop(0, tiles, step, 0)
+        lax.fori_loop(cuts[p] // tile, cuts[p + 1] // tile, step, 0)
 
     def cols(p):
         return pl.ds(cuts[p], cuts[p + 1] - cuts[p])
@@ -221,10 +226,9 @@
             device_id=mate, device_id_type=MESH,
         )
 
-    def pair_send(phase):
+    def pair_send(phase, p):
         yy = (y1 + phase) % NY
-        for p in range(2):
-            send(None, functools.partial(pair_copy, yy, p))
+        send(None, functools.partial(pair_copy, yy, p))
 
     def pair_add(phase, p):
         yy = (y1 + phase) % NY
@@ -267,13 +271,22 @@
         got = rz_a[way, t] if p == 0 else rz_b[yy, way, t]
         part[blk(yy, c, t), :, cols(p)] += got
 
+    def line_edge(p, yy, cond=None):
+        for on, way, order in (
+            (z == 0, UP, range(nd - 1, 0, -1)),
+            (z == nd - 1, DOWN, range(nd - 1)),
+        ):
+            on = on if cond is None else both(cond, on)
+            for t in order:
+                send(on, functools.partial(line_copy, p, yy, t, way))
+
     def line_step(p, yy, s, cond=None):
         for t, way, mine, more in (
             (nd - 1 - s, UP, z < nd - 1 - s, has_down),
             (s, DOWN, z > s, has_up),
         ):
-            on = mine if cond is None else both(cond, mine)
-            pl.when(both(on, more))(functools.partial(line_take, p, yy, t, way))
+            on = both(mine, more) if cond is None else both(cond, both(mine, more))
+            pl.when(on)(functools.partial(line_take, p, yy, t, way))
             send(on, functools.partial(line_copy, p, yy, t, way))
 
     def line_end(p, yy, cond=None):
@@ -291,49 +304,57 @@
     y2 = (y1 + 1) % NY
     first, second = y == y1, y != y1
 
-    partial(0)
-    pair_send(0)
+    prepare(0)
+    for p in range(2):
+        partial(0, p)
+        pair_send(0, p)
+    pair_add(0, 0)
+    across_send(0)
     ag_cross(1, 0)
     ag_line(0, y, 1)
     ag_line(1, y, 1)
-    pair_add(0, 0)
-    across_send(0)
     pair_add(0, 1)
-    line_step(1, y1, 0)
-    ag_cross(0, 0)
+    line_edge(1, y1)
+    prepare(1)
+    partial(1, 0)
+    pair_send(1, 0)
     ag_cross(1, 1)
     ag_line(0, y, 2)
     ag_line(1, y, 2)
-    partial(1)
-    pair_send(1)
-    line_step(1, y1, 1)
+    partial(1, 1)
+    pair_send(1, 1)
     pair_add(1, 0)
     across_send(1)
     pair_add(1, 1)
-    line_step(1, y2, 0)
+    line_edge(1, y2)
+    line_step(1, y1, 0)
+    ag_cross(0, 0)
     for s in range(3, nd):
         ag_line(0, y, s)
         ag_line(1, y, s)
     for s in range(2, nd):
         ag_cross(1, s)
     pl.when(first)(across_add)
+    line_edge(0, y, first)
+    line_step(1, y1, 1)
     line_step(0, y, 0, first)
+    line_step(1, y2, 0)
     for s in range(2, nd - 1):
         line_step(1, y1, s)
+    line_end(1, y1)
+    send(second, last_copy)
     line_step(0, y, 1, first)
     line_step(1, y2, 1)
-    line_end(1, y1)
-    send(second, last_copy)
     pl.when(second)(across_add)
+    line_edge(0, y, second)
     line_step(0, y, 0, second)
     for s in range(2, nd - 1):
         line_step(0, y, s, first)
     for s in range(2, nd - 1):
         line_step(1, y2, s)
-    line_step(0, y, 1, second)
     line_end(1, y2)
     send(first, last_copy)
-    for s in range(2, nd - 1):
+    for s in range(1, nd - 1):
         line_step(0, y, s, second)
 
     for s in range(1, nd):
@@ -343,12 +364,21 @@
             for zz in range(nd):
                 ag_wait(None, p, blk(yy, oc, zz))
 
+    def turned_copies(i):
+        at = pl.ds(pl.multiple_of(i * tile, tile), tile)
+        return (
+            pltpu.make_async_copy(th.at[at, :], ath_ref.at[at, :], t_sem.at[0, i]),
+            pltpu.make_async_copy(tl.at[at, :], atl_ref.at[at, :], t_sem.at[1, i]),
+        )
+
     def turn(i, carry):
         at = pl.ds(pl.multiple_of(i * tile, tile), tile)
         block = acts[:, :, at].reshape(2 * NY * nd * tb, tile)
         high, low = split(block.T)
-        ath_ref[at, :] = high
-        atl_ref[at, :] = low
+        th[at, :] = high
+        tl[at, :] = low
+        for copy in turned_copies(i):
+            copy.start()
         return carry
 
     lax.fori_loop(0, tiles, turn, 0)
@@ -358,6 +388,9 @@
     part[me, :, cols(1)] += ry_b[...]
     out_ref[...] = part[me]
 
+    for i in range(tiles):
+        for copy in turned_copies(i):
+            copy.wait()
     for cond, make in started:
         if cond is None:
             make().wait_send()
@@ -366,25 +399,22 @@
 
 
 def weight_kernel(ath_ref, atl_ref, gh_ref, gl_ref, out_ref):
-    def dot(a, b):
-        return jnp.dot(a, b, preferred_element_type=jnp.float32)
-
-    high = ath_ref[...]
-    out_ref[...] = dot(high, gh_ref[...]) + (
-        dot(high, gl_ref[...]) + dot(atl_ref[...], gh_ref[...])
-    )
+    high, g_high = ath_ref[...], gh_ref[...]
+    left = jnp.concatenate([high, atl_ref[...], high], axis=1)
+    right = jnp.concatenate([g_high, g_high, gl_ref[...]], axis=0)
+    out_ref[...] = jnp.dot(left, right, preferred_element_type=jnp.float32)
 
 
 def shards(rows, nc, nd, activations, grad_output, up_weight):
     tb, dm = activations.shape
     trow, df = grad_output.shape
     tokens = trow * rows
-    tile = min(512, dm)
+    tile = max(128, dm // 8)
     f32, bf16 = jnp.float32, jnp.bfloat16
-    step = max(128, dm // 8)
-    cuts = (0, (dm // step * 5 // 8) * step, dm)
+    cuts = (0, (dm // tile * 5 // 8) * tile, dm)
     wa, wb = cuts[1], dm - cuts[1]
     vmem = pl.BlockSpec(memory_space=pltpu.VMEM)
+    hbm = pl.BlockSpec(memory_space=pl.ANY)
     dma = pltpu.SemaphoreType.DMA
     grad_input, ath, atl, gh, gl = pl.pallas_call(
         functools.partial(exchange_kernel, rows, nd, cuts, tile),
@@ -395,11 +425,14 @@
             jax.ShapeDtypeStruct((tokens, df), bf16),
             jax.ShapeDtypeStruct((tokens, df), bf16),
         ),
-        in_specs=[vmem, vmem, pl.BlockSpec(memory_space=pl.ANY)],
-        out_specs=(vmem,) * 5,
+        in_specs=[vmem, vmem, hbm],
+        out_specs=(vmem, hbm, hbm, vmem, vmem),
         scratch_shapes=[
             pltpu.VMEM((nc * nd, tb, dm), f32),
             pltpu.VMEM((rows, trow, df), f32),
+            pltpu.VMEM((NY, 2 * tokens // NY, df), bf16),
+            pltpu.VMEM((dm, tokens), bf16),
+            pltpu.VMEM((dm, tokens), bf16),
             pltpu.VMEM((min(3, dm // tile), tile, df), f32),
             pltpu.VMEM((dm, df), bf16),
             pltpu.VMEM((dm, df), bf16),
@@ -409,6 +442,7 @@
             pltpu.VMEM((tb, wb), f32),
             pltpu.VMEM((2, nd, tb, wa), f32),
             pltpu.VMEM((NY, 2, nd, tb, wb), f32),
+            dma((2, dm // tile)),
             dma((3,)),
             dma((rows,)),
             dma((rows,)),
@@ -426,7 +460,7 @@
             dma((NY, 2, nd)),
         ],
         compiler_params=pltpu.CompilerParams(
-            collective_id=0, has_side_effects=True, vmem_limit_bytes=60 * 2**20
+            collective_id=0, has_side_effects=True, vmem_limit_bytes=62 * 2**20
         ),
         cost_estimate=pl.CostEstimate(
             flops=6 * tokens * dm * df, bytes_accessed=4 * dm * df, transcendentals=0
@@ -445,7 +479,7 @@
             pl.BlockSpec((tokens, df), lambda i: (0, 0)),
         ],
         out_specs=pl.BlockSpec((tile, df), lambda i: (i, 0)),
-        compiler_params=pltpu.CompilerParams(vmem_limit_bytes=48 * 2**20),
+        compiler_params=pltpu.CompilerParams(vmem_limit_bytes=63 * 2**20),
         cost_estimate=pl.CostEstimate(
             flops=6 * tokens * dm * df, bytes_accessed=4 * dm * df, transcendentals=0
         ),

time: 100 us -> 86.6 us (0.87)
  Pallas kernels: 92.8 us -> 84.8 us
  local copies, waits for them, and re-layouts: 5.96 us -> 0.71 us
    pallas_call x1, Pallas kernels: 82.6 us -> 72.5 us  [shards(): pl.pallas_call(functools.partial(exchange_kernel, rows, nd, cuts, tile),...]
    unnamed x11 -> x3, local copies, waits for them, and re-layouts: 5.96 us -> 0.71 us
    pallas_call x1, Pallas kernels: 10.2 us -> 12.3 us  [shards(): pl.pallas_call(weight_kernel, grid=(dm // tile,), out_shape=jax.ShapeDtyp...]
where the time goes in v2:
time: 86.6 us; the launch traced here: 86.2 us
  Pallas kernels  84.8 us (98%)
    pallas_call x1, Pallas kernels, shards(): pl.pallas_call(functools.partial(exchange_kernel, rows, nd, cuts, tile),...  72.5 us
    pallas_call x1, Pallas kernels, shards(): pl.pallas_call(weight_kernel, grid=(dm // tile,), out_shape=jax.ShapeDtyp...  12.3 us

profile of v2, /device:TPU:17, one launch (start us, length us, event | category | flops | bytes accessed | tf_op | source)
XLA Modules:
  0.0 86.2 jit_solution(18404697070151294348)
XLA Ops:
  0.6 72.5 %exchange.1 = (f32[16,4096]{1,0:T(8,128)}, bf16[4096,256]{1,0:T(8,128)(2,1)}, bf16[4096,256]{1,0:T(8,128)(2,1)}, bf16[256,1024]{1,0:T(8,128)(2,1)}, bf16[256,1024]{1,0:T(8,128)(2,1)}) custom-call(f32[16,4096]{1,0:T(8,128)} %acts_ref.1, f32[128,1024]{1,0:T(8,128)} %grads_ref.1, f32[4096,1024]{1,0:T(8,128)} %weight_ref.1), custom_call_target="tpu_custom_call" | custom-call | flops 6442450944 | bytes 16777216 | tf_op jit(solution)/shard_map/exchange/pallas_call | solution.py:419
  73.2 0.0 copy-start
  73.2 12.3 %weight_grad.1 = f32[4096,1024]{1,0:T(8,128)} custom-call(bf16[4096,256]{1,0:T(8,128)(2,1)} %get-tuple-element.8.ath_ref, bf16[4096,256]{1,0:T(8,128)(2,1)} %get-tuple-element.9.atl_ref, bf16[256,1024]{1,0:T(8,128)(2,1)} %get-tuple-element.10.gh_ref, bf16[256,1024]{1,0:T(8,128)(2,1)} %get-tuple-element.11.gl_ref), custom_call_target="tpu_custom_call" | custom-call | flops 6442450944 | bytes 16777216 | tf_op jit(solution)/shard_map/weight_grad/pallas_call | solution.py:471
  85.5 0.0 copy-done
  85.5 0.7 copy.6
Async XLA Ops:
  73.2 12.3 %copy-start = (f32[16,4096]{1,0:T(8,128)S(1)}, f32[16,4096]{1,0:T(8,128)}, u32[]{:S(2)}) copy-start(f32[16,4096]{1,0:T(8,128)} %get-tuple-element.14) | copy-start | bytes 786436

commit v3 on v2

--- a/solution.py
+++ b/solution.py
@@ -31,8 +31,8 @@
 def exchange_kernel(
     rows, nd, cuts, tile,
     acts_ref, grads_ref, weight_ref,
-    out_ref, ath_ref, atl_ref, gh_ref, gl_ref,
-    acts, grads, gcat, th, tl, stage, wh, wl, part, rc, ry_a, ry_b, rz_a, rz_b,
+    out_ref, left_ref, right_ref,
+    acts, grads, turned, stage, wh, wl, part, rc, ry_a, ry_b, rz_a, rz_b,
     t_sem, w_sem, x_s, x_r, ag_s, ag_r, c_s, c_r, ya_s, ya_r, yb_s, yb_r, za_s, za_r, zb_s, zb_r,
 ):
     x = lax.axis_index("row")
@@ -183,11 +183,11 @@
                 ).wait_recv()
 
             high, low = split(grads[q])
-            at = pl.ds(pl.multiple_of(q * trow, trow), trow)
-            gh_ref[at, :] = high
-            gl_ref[at, :] = low
-            gcat[phase, j * trow : (j + 1) * trow, :] = high
-            gcat[phase, half + j * trow : half + (j + 1) * trow, :] = low
+            at = pl.multiple_of(yy * 2 * half + j * trow, trow)
+            right_ref[pl.ds(at, trow), :] = high
+            right_ref[pl.ds(pl.multiple_of(at + half, trow), trow), :] = low
+            extra = pl.multiple_of(2 * NY * half + q * trow, trow)
+            right_ref[pl.ds(extra, trow), :] = high
 
     def partial(phase, p):
         yy = (y1 + phase) % NY
@@ -206,8 +206,10 @@
                     weight_copy(i + slots, slot).start()
             else:
                 high, low = wh[rows_at, :], wl[rows_at, :]
-            pairs = dot_nt(gcat[phase], high)
-            total = pairs[:half] + (pairs[half:] + dot_nt(gcat[phase, :half, :], low))
+            at = pl.multiple_of(yy * 2 * half, half)
+            pairs = dot_nt(right_ref[pl.ds(at, 2 * half), :], high)
+            crossed = dot_nt(right_ref[pl.ds(at, half), :], low)
+            total = pairs[:half] + (pairs[half:] + crossed)
             part[pl.ds(yy * 2 * nd, 2 * nd), :, rows_at] = total.reshape(
                 2 * nd, tb, tile
             )
@@ -245,15 +247,19 @@
 
     def across_send(phase):
         yy = (y1 + phase) % NY
-        order = sorted(range(nd), key=lambda t: -abs(2 * t - nd + 1))
-        for t in order:
-            send(yy != y, functools.partial(across_copy, t))
-
-    def across_add():
-        order = sorted(range(nd), key=lambda t: -abs(2 * t - nd + 1))
-        for t in order:
-            across_copy(t).wait_recv()
-            part[blk(y, c, t), :, cols(0)] += ry_a[t]
+        for zz in range(nd):
+
+            @pl.when(both(yy != y, z == zz))
+            def _(zz=zz):
+                for t in sorted(range(nd), key=lambda t: -abs(t - zz)):
+                    across_copy(t).start()
+
+        for t in range(nd):
+            started.append((yy != y, functools.partial(across_copy, t)))
+
+    def across_take(t):
+        across_copy(t).wait_recv()
+        part[blk(y, c, t), :, cols(0)] += ry_a[t]
 
     def line_copy(p, yy, t, way):
         if p == 0:
@@ -278,6 +284,8 @@
         ):
             on = on if cond is None else both(cond, on)
             for t in order:
+                if p == 0:
+                    pl.when(on)(functools.partial(across_take, t))
                 send(on, functools.partial(line_copy, p, yy, t, way))
 
     def line_step(p, yy, s, cond=None):
@@ -286,6 +294,8 @@
             (s, DOWN, z > s, has_up),
         ):
             on = both(mine, more) if cond is None else both(cond, both(mine, more))
+            if p == 0:
+                pl.when(on)(functools.partial(across_take, t))
             pl.when(on)(functools.partial(line_take, p, yy, t, way))
             send(on, functools.partial(line_copy, p, yy, t, way))
 
@@ -316,81 +326,74 @@
     pair_add(0, 1)
     line_edge(1, y1)
     prepare(1)
-    partial(1, 0)
-    pair_send(1, 0)
+    for p in range(2):
+        partial(1, p)
+        pair_send(1, p)
+    pair_add(1, 0)
+    across_send(1)
     ag_cross(1, 1)
     ag_line(0, y, 2)
     ag_line(1, y, 2)
-    partial(1, 1)
-    pair_send(1, 1)
-    pair_add(1, 0)
-    across_send(1)
     pair_add(1, 1)
     line_edge(1, y2)
+    line_edge(0, y, first)
     line_step(1, y1, 0)
+    line_step(0, y, 0, first)
     ag_cross(0, 0)
     for s in range(3, nd):
         ag_line(0, y, s)
         ag_line(1, y, s)
     for s in range(2, nd):
         ag_cross(1, s)
-    pl.when(first)(across_add)
-    line_edge(0, y, first)
-    line_step(1, y1, 1)
-    line_step(0, y, 0, first)
     line_step(1, y2, 0)
-    for s in range(2, nd - 1):
-        line_step(1, y1, s)
-    line_end(1, y1)
-    send(second, last_copy)
-    line_step(0, y, 1, first)
-    line_step(1, y2, 1)
-    pl.when(second)(across_add)
     line_edge(0, y, second)
     line_step(0, y, 0, second)
-    for s in range(2, nd - 1):
+    for s in range(1, nd - 1):
+        line_step(1, y1, s)
         line_step(0, y, s, first)
-    for s in range(2, nd - 1):
+        if s == nd - 2:
+            line_end(1, y1)
+            send(second, last_copy)
         line_step(1, y2, s)
+        line_step(0, y, s, second)
+        if s == 1:
+            ag_cross(0, 1)
     line_end(1, y2)
     send(first, last_copy)
-    for s in range(1, nd - 1):
-        line_step(0, y, s, second)
-
-    for s in range(1, nd):
+
+    for s in range(2, nd):
         ag_cross(0, s)
     for p in range(2):
         for yy in range(NY):
             for zz in range(nd):
                 ag_wait(None, p, blk(yy, oc, zz))
 
-    def turned_copies(i):
+    def turned_copy(i):
         at = pl.ds(pl.multiple_of(i * tile, tile), tile)
-        return (
-            pltpu.make_async_copy(th.at[at, :], ath_ref.at[at, :], t_sem.at[0, i]),
-            pltpu.make_async_copy(tl.at[at, :], atl_ref.at[at, :], t_sem.at[1, i]),
-        )
+        return pltpu.make_async_copy(turned.at[at, :], left_ref.at[at, :], t_sem.at[i])
 
     def turn(i, carry):
         at = pl.ds(pl.multiple_of(i * tile, tile), tile)
         block = acts[:, :, at].reshape(2 * NY * nd * tb, tile)
         high, low = split(block.T)
-        th[at, :] = high
-        tl[at, :] = low
-        for copy in turned_copies(i):
-            copy.start()
+        for yy in range(NY):
+            own = high[:, yy * half : (yy + 1) * half]
+            turned[at, 2 * yy * half : (2 * yy + 1) * half] = own
+            turned[at, (2 * yy + 1) * half : (2 * yy + 2) * half] = own
+        turned[at, 2 * NY * half :] = low
+        turned_copy(i).start()
         return carry
 
     lax.fori_loop(0, tiles, turn, 0)
 
+    across_take(z)
     line_end(0, y)
     last_copy().wait_recv()
     part[me, :, cols(1)] += ry_b[...]
     out_ref[...] = part[me]
 
     for i in range(tiles):
-        for copy in turned_copies(i):
-            copy.wait()
+        turned_copy(i).wait()
     for cond, make in started:
         if cond is None:
             make().wait_send()
@@ -398,11 +401,10 @@
             pl.when(cond)(lambda make=make: make().wait_send())
 
 
-def weight_kernel(ath_ref, atl_ref, gh_ref, gl_ref, out_ref):
-    high, g_high = ath_ref[...], gh_ref[...]
-    left = jnp.concatenate([high, atl_ref[...], high], axis=1)
-    right = jnp.concatenate([g_high, g_high, gl_ref[...]], axis=0)
-    out_ref[...] = jnp.dot(left, right, preferred_element_type=jnp.float32)
+def weight_kernel(left_ref, right_ref, out_ref):
+    out_ref[...] = jnp.dot(
+        left_ref[...], right_ref[...], preferred_element_type=jnp.float32
+    )
 
 
 def shards(rows, nc, nd, activations, grad_output, up_weight):
@@ -416,23 +418,19 @@
     vmem = pl.BlockSpec(memory_space=pltpu.VMEM)
     hbm = pl.BlockSpec(memory_space=pl.ANY)
     dma = pltpu.SemaphoreType.DMA
-    grad_input, ath, atl, gh, gl = pl.pallas_call(
+    grad_input, left, right = pl.pallas_call(
         functools.partial(exchange_kernel, rows, nd, cuts, tile),
         out_shape=(
             jax.ShapeDtypeStruct((tb, dm), f32),
-            jax.ShapeDtypeStruct((dm, tokens), bf16),
-            jax.ShapeDtypeStruct((dm, tokens), bf16),
-            jax.ShapeDtypeStruct((tokens, df), bf16),
-            jax.ShapeDtypeStruct((tokens, df), bf16),
+            jax.ShapeDtypeStruct((dm, 3 * tokens), bf16),
+            jax.ShapeDtypeStruct((3 * tokens, df), bf16),
         ),
         in_specs=[vmem, vmem, hbm],
-        out_specs=(vmem, hbm, hbm, vmem, vmem),
+        out_specs=(vmem, hbm, vmem),
         scratch_shapes=[
             pltpu.VMEM((nc * nd, tb, dm), f32),
             pltpu.VMEM((rows, trow, df), f32),
-            pltpu.VMEM((NY, 2 * tokens // NY, df), bf16),
-            pltpu.VMEM((dm, tokens), bf16),
-            pltpu.VMEM((dm, tokens), bf16),
+            pltpu.VMEM((dm, 3 * tokens), bf16),
             pltpu.VMEM((min(3, dm // tile), tile, df), f32),
             pltpu.VMEM((dm, df), bf16),
             pltpu.VMEM((dm, df), bf16),
@@ -442,7 +440,7 @@
             pltpu.VMEM((tb, wb), f32),
             pltpu.VMEM((2, nd, tb, wa), f32),
             pltpu.VMEM((NY, 2, nd, tb, wb), f32),
-            dma((2, dm // tile)),
+            dma((dm // tile,)),
             dma((3,)),
             dma((rows,)),
             dma((rows,)),
@@ -473,10 +471,8 @@
         grid=(dm // tile,),
         out_shape=jax.ShapeDtypeStruct((dm, df), f32),
         in_specs=[
-            pl.BlockSpec((tile, tokens), lambda i: (i, 0)),
-            pl.BlockSpec((tile, tokens), lambda i: (i, 0)),
-            pl.BlockSpec((tokens, df), lambda i: (0, 0)),
-            pl.BlockSpec((tokens, df), lambda i: (0, 0)),
+            pl.BlockSpec((tile, 3 * tokens), lambda i: (i, 0)),
+            pl.BlockSpec((3 * tokens, df), lambda i: (0, 0)),
         ],
         out_specs=pl.BlockSpec((tile, df), lambda i: (i, 0)),
         compiler_params=pltpu.CompilerParams(vmem_limit_bytes=63 * 2**20),
@@ -484,7 +480,7 @@
             flops=6 * tokens * dm * df, bytes_accessed=4 * dm * df, transcendentals=0
         ),
         name="weight_grad",
-    )(ath, atl, gh, gl)
+    )(left, right)
     return grad_input, grad_weight
 
 

time: 86.6 us -> 84.2 us (0.972)
  Pallas kernels: 84.8 us -> 82.5 us
    pallas_call x1, Pallas kernels: 72.5 us -> 69 us  [shards(): pl.pallas_call(functools.partial(exchange_kernel, rows, nd, cuts, tile),...]
    pallas_call x1, Pallas kernels: 12.3 us -> 13.5 us  [shards(): pl.pallas_call(weight_kernel, grid=(dm // tile,), out_shape=jax.ShapeDtyp...]
where the time goes in v3:
time: 84.2 us; the launch traced here: 83.8 us
  Pallas kernels  82.5 us (98%)
    pallas_call x1, Pallas kernels, shards(): pl.pallas_call(functools.partial(exchange_kernel, rows, nd, cuts, tile),...  69 us
    pallas_call x1, Pallas kernels, shards(): pl.pallas_call(weight_kernel, grid=(dm // tile,), out_shape=jax.ShapeDtyp...  13.5 us

profile of v3, /device:TPU:17, one launch (start us, length us, event | category | flops | bytes accessed | tf_op | source)
XLA Modules:
  0.0 83.8 jit_solution(8588443041265127224)
XLA Ops:
  0.6 69.0 %exchange.1 = (f32[16,4096]{1,0:T(8,128)}, bf16[4096,768]{1,0:T(8,128)(2,1)}, bf16[768,1024]{1,0:T(8,128)(2,1)}) custom-call(f32[16,4096]{1,0:T(8,128)} %acts_ref.1, f32[128,1024]{1,0:T(8,128)} %grads_ref.1, f32[4096,1024]{1,0:T(8,128)} %weight_ref.1), custom_call_target="tpu_custom_call" | custom-call | flops 6442450944 | bytes 16777216 | tf_op jit(solution)/shard_map/exchange/pallas_call | solution.py:421
  69.6 0.0 copy-start
  69.6 13.5 %weight_grad.1 = f32[4096,1024]{1,0:T(8,128)} custom-call(bf16[4096,768]{1,0:T(8,128)(2,1)} %get-tuple-element.6.left_ref, bf16[768,1024]{1,0:T(8,128)(2,1)} %get-tuple-element.7.right_ref), custom_call_target="tpu_custom_call" | custom-call | flops 6442450944 | bytes 16777216 | tf_op jit(solution)/shard_map/weight_grad/pallas_call | solution.py:469
  83.1 0.0 copy-done
  83.1 0.7 copy.6
Async XLA Ops:
  69.6 13.5 %copy-start = (f32[16,4096]{1,0:T(8,128)S(1)}, f32[16,4096]{1,0:T(8,128)}, u32[]{:S(2)}) copy-start(f32[16,4096]{1,0:T(8,128)} %get-tuple-element.10) | copy-start | bytes 786436

commit v4 on v3

--- a/solution.py
+++ b/solution.py
@@ -31,8 +31,8 @@
 def exchange_kernel(
     rows, nd, cuts, tile,
     acts_ref, grads_ref, weight_ref,
-    out_ref, left_ref, right_ref,
-    acts, grads, turned, stage, wh, wl, part, rc, ry_a, ry_b, rz_a, rz_b,
+    out_ref, feats_ref, grads_out_ref,
+    acts, grads, gcat, stage, wh, wl, part, rc, ry_a, ry_b, rz_a, rz_b,
     t_sem, w_sem, x_s, x_r, ag_s, ag_r, c_s, c_r, ya_s, ya_r, yb_s, yb_r, za_s, za_r, zb_s, zb_r,
 ):
     x = lax.axis_index("row")
@@ -183,13 +183,10 @@
                 ).wait_recv()
 
             high, low = split(grads[q])
-            at = pl.multiple_of(yy * 2 * half + j * trow, trow)
-            right_ref[pl.ds(at, trow), :] = high
-            right_ref[pl.ds(pl.multiple_of(at + half, trow), trow), :] = low
-            extra = pl.multiple_of(2 * NY * half + q * trow, trow)
-            right_ref[pl.ds(extra, trow), :] = high
-
-    def partial(phase, p):
+            gcat[phase, j * trow : (j + 1) * trow, :] = high
+            gcat[phase, half + j * trow : half + (j + 1) * trow, :] = low
+
+    def partial(phase, begin, end):
         yy = (y1 + phase) % NY
 
         def step(i, carry):
@@ -206,16 +203,15 @@
                     weight_copy(i + slots, slot).start()
             else:
                 high, low = wh[rows_at, :], wl[rows_at, :]
-            at = pl.multiple_of(yy * 2 * half, half)
-            pairs = dot_nt(right_ref[pl.ds(at, 2 * half), :], high)
-            crossed = dot_nt(right_ref[pl.ds(at, half), :], low)
+            pairs = dot_nt(gcat[phase], high)
+            crossed = dot_nt(gcat[phase, :half, :], low)
             total = pairs[:half] + (pairs[half:] + crossed)
             part[pl.ds(yy * 2 * nd, 2 * nd), :, rows_at] = total.reshape(
                 2 * nd, tb, tile
             )
             return carry
 
-        lax.fori_loop(cuts[p] // tile, cuts[p + 1] // tile, step, 0)
+        lax.fori_loop(begin, end, step, 0)
 
     def cols(p):
         return pl.ds(cuts[p], cuts[p + 1] - cuts[p])
@@ -314,35 +310,47 @@
     y2 = (y1 + 1) % NY
     first, second = y == y1, y != y1
 
+    def grads_copy():
+        return pltpu.make_async_copy(grads, grads_out_ref, t_sem.at[0])
+
+    def feats_copy():
+        return pltpu.make_async_copy(acts, feats_ref, t_sem.at[1])
+
+    middle = cuts[1] // tile
+    some = (middle + 1) // 2
     prepare(0)
-    for p in range(2):
-        partial(0, p)
-        pair_send(0, p)
-    pair_add(0, 0)
-    across_send(0)
+    partial(0, 0, middle)
+    pair_send(0, 0)
     ag_cross(1, 0)
     ag_line(0, y, 1)
     ag_line(1, y, 1)
-    pair_add(0, 1)
-    line_edge(1, y1)
+    pair_add(0, 0)
+    across_send(0)
+    partial(0, middle, tiles)
+    pair_send(0, 1)
     prepare(1)
-    for p in range(2):
-        partial(1, p)
-        pair_send(1, p)
-    pair_add(1, 0)
-    across_send(1)
+    grads_copy().start()
+    partial(1, 0, some)
     ag_cross(1, 1)
     ag_line(0, y, 2)
     ag_line(1, y, 2)
+    pair_add(0, 1)
+    line_edge(1, y1)
+    partial(1, some, middle)
+    pair_send(1, 0)
+    pair_add(1, 0)
+    across_send(1)
+    partial(1, middle, tiles)
+    pair_send(1, 1)
+    ag_cross(0, 0)
+    for s in range(3, nd):
+        ag_line(0, y, s)
+        ag_line(1, y, s)
     pair_add(1, 1)
     line_edge(1, y2)
     line_edge(0, y, first)
     line_step(1, y1, 0)
     line_step(0, y, 0, first)
-    ag_cross(0, 0)
-    for s in range(3, nd):
-        ag_line(0, y, s)
-        ag_line(1, y, s)
     for s in range(2, nd):
         ag_cross(1, s)
     line_step(1, y2, 0)
@@ -368,23 +376,7 @@
             for zz in range(nd):
                 ag_wait(None, p, blk(yy, oc, zz))
 
-    def turned_copy(i):
-        at = pl.ds(pl.multiple_of(i * tile, tile), tile)
-        return pltpu.make_async_copy(turned.at[at, :], left_ref.at[at, :], t_sem.at[i])
-
-    def turn(i, carry):
-        at = pl.ds(pl.multiple_of(i * tile, tile), tile)
-        block = acts[:, :, at].reshape(2 * NY * nd * tb, tile)
-        high, low = split(block.T)
-        for yy in range(NY):
-            own = high[:, yy * half : (yy + 1) * half]
-            turned[at, 2 * yy * half : (2 * yy + 1) * half] = own
-            turned[at, (2 * yy + 1) * half : (2 * yy + 2) * half] = own
-        turned[at, 2 * NY * half :] = low
-        turned_copy(i).start()
-        return carry
-
-    lax.fori_loop(0, tiles, turn, 0)
+    feats_copy().start()
 
     across_take(z)
     line_end(0, y)
@@ -392,19 +384,13 @@
     part[me, :, cols(1)] += ry_b[...]
     out_ref[...] = part[me]
 
-    for i in range(tiles):
-        turned_copy(i).wait()
+    grads_copy().wait()
+    feats_copy().wait()
     for cond, make in started:
         if cond is None:
             make().wait_send()
         else:
             pl.when(cond)(lambda make=make: make().wait_send())
-
-
-def weight_kernel(left_ref, right_ref, out_ref):
-    out_ref[...] = jnp.dot(
-        left_ref[...], right_ref[...], preferred_element_type=jnp.float32
-    )
 
 
 def shards(rows, nc, nd, activations, grad_output, up_weight):
@@ -418,19 +404,19 @@
     vmem = pl.BlockSpec(memory_space=pltpu.VMEM)
     hbm = pl.BlockSpec(memory_space=pl.ANY)
     dma = pltpu.SemaphoreType.DMA
-    grad_input, left, right = pl.pallas_call(
+    grad_input, feats, grads = pl.pallas_call(
         functools.partial(exchange_kernel, rows, nd, cuts, tile),
         out_shape=(
             jax.ShapeDtypeStruct((tb, dm), f32),
-            jax.ShapeDtypeStruct((dm, 3 * tokens), bf16),
-            jax.ShapeDtypeStruct((3 * tokens, df), bf16),
+            jax.ShapeDtypeStruct((nc * nd, tb, dm), f32),
+            jax.ShapeDtypeStruct((rows, trow, df), f32),
         ),
         in_specs=[vmem, vmem, hbm],
-        out_specs=(vmem, hbm, vmem),
+        out_specs=(vmem, hbm, hbm),
         scratch_shapes=[
             pltpu.VMEM((nc * nd, tb, dm), f32),
             pltpu.VMEM((rows, trow, df), f32),
-            pltpu.VMEM((dm, 3 * tokens), bf16),
+            pltpu.VMEM((NY, 2 * tokens // NY, df), bf16),
             pltpu.VMEM((min(3, dm // tile), tile, df), f32),
             pltpu.VMEM((dm, df), bf16),
             pltpu.VMEM((dm, df), bf16),
@@ -440,7 +426,7 @@
             pltpu.VMEM((tb, wb), f32),
             pltpu.VMEM((2, nd, tb, wa), f32),
             pltpu.VMEM((NY, 2, nd, tb, wb), f32),
-            dma((dm // tile,)),
+            dma((2,)),
             dma((3,)),
             dma((rows,)),
             dma((rows,)),
@@ -466,21 +452,13 @@
         name="exchange",
     )(activations, grad_output, up_weight)
 
-    grad_weight = pl.pallas_call(
-        weight_kernel,
-        grid=(dm // tile,),
-        out_shape=jax.ShapeDtypeStruct((dm, df), f32),
-        in_specs=[
-            pl.BlockSpec((tile, 3 * tokens), lambda i: (i, 0)),
-            pl.BlockSpec((3 * tokens, df), lambda i: (0, 0)),
-        ],
-        out_specs=pl.BlockSpec((tile, df), lambda i: (i, 0)),
-        compiler_params=pltpu.CompilerParams(vmem_limit_bytes=63 * 2**20),
-        cost_estimate=pl.CostEstimate(
-            flops=6 * tokens * dm * df, bytes_accessed=4 * dm * df, transcendentals=0
-        ),
-        name="weight_grad",
-    )(left, right)
+    grad_weight = lax.dot_general(
+        feats.reshape(tokens, dm),
+        grads.reshape(tokens, df),
+        (((0,), (0,)), ((), ())),
+        precision=lax.Precision.HIGH,
+        preferred_element_type=f32,
+    )
     return grad_input, grad_weight
 
 

time: 84.2 us -> 84 us (level)
  matrix products: 0 us -> 12.3 us
  Pallas kernels: 82.5 us -> 70.2 us
    pallas_call x1 -> x0, Pallas kernels: 13.5 us -> none  [shards(): pl.pallas_call(weight_kernel, grid=(dm // tile,), out_shape=jax.ShapeDtyp...]
    dot_general x0 -> x1, matrix products: none -> 12.3 us  [shards(): lax.dot_general(feats.reshape(tokens, dm), grads.reshape(tokens, df), (((...]
    pallas_call x1, Pallas kernels: 69 us -> 70.2 us  [shards(): pl.pallas_call(functools.partial(exchange_kernel, rows, nd, cuts, tile),...]
where the time goes in v4:
time: 84 us; the launch traced here: 83.9 us
  Pallas kernels  70.2 us (84%)
  matrix products  12.3 us (15%)
    pallas_call x1, Pallas kernels, shards(): pl.pallas_call(functools.partial(exchange_kernel, rows, nd, cuts, tile),...  70.2 us
    dot_general x1, matrix products, shards(): lax.dot_general(feats.reshape(tokens, dm), grads.reshape(tokens, df), (((...  12.3 us

profile of v4, /device:TPU:17, one launch (start us, length us, event | category | flops | bytes accessed | tf_op | source)
XLA Modules:
  0.0 83.9 jit_solution(8115253603214498134)
XLA Ops:
  0.6 70.2 %exchange.1 = (f32[16,4096]{1,0:T(8,128)}, f32[16,16,4096]{2,1,0:T(8,128)}, f32[2,128,1024]{2,1,0:T(8,128)}) custom-call(f32[16,4096]{1,0:T(8,128)} %acts_ref.1, f32[128,1024]{1,0:T(8,128)} %grads_ref.1, f32[4096,1024]{1,0:T(8,128)} %weight_ref.1), custom_call_target="tpu_custom_call" | custom-call | flops 6442450944 | bytes 16777216 | tf_op jit(solution)/shard_map/exchange/pallas_call | solution.py:407
  70.8 0.0 copy-start
  70.9 12.3 %fusion = f32[4096,1024]{1,0:T(8,128)} fusion(f32[256,4096]{1,0:T(8,128)} %bitcast.4, f32[256,1024]{1,0:T(8,128)} %bitcast.5), kind=kOutput, calls=%fused_computation | convolution fusion | flops 6442450944 | bytes 22020096 | tf_op jit(solution)/shard_map/dot_general | solution.py:455
  83.1 0.0 copy-done
  83.2 0.7 copy.6
Async XLA Ops:
  70.8 12.3 %copy-start = (f32[16,4096]{1,0:T(8,128)S(1)}, f32[16,4096]{1,0:T(8,128)}, u32[]{:S(2)}) copy-start(f32[16,4096]{1,0:T(8,128)} %get-tuple-element.10) | copy-start | bytes 786436

commit v5 on v4

--- a/solution.py
+++ b/solution.py
@@ -330,27 +330,27 @@
     pair_send(0, 1)
     prepare(1)
     grads_copy().start()
+    pair_add(0, 1)
+    line_edge(1, y1)
     partial(1, 0, some)
     ag_cross(1, 1)
     ag_line(0, y, 2)
     ag_line(1, y, 2)
-    pair_add(0, 1)
-    line_edge(1, y1)
     partial(1, some, middle)
     pair_send(1, 0)
     pair_add(1, 0)
     across_send(1)
-    partial(1, middle, tiles)
-    pair_send(1, 1)
-    ag_cross(0, 0)
+    line_edge(0, y, first)
+    line_step(1, y1, 0)
     for s in range(3, nd):
         ag_line(0, y, s)
         ag_line(1, y, s)
+    partial(1, middle, tiles)
+    pair_send(1, 1)
+    line_step(0, y, 0, first)
     pair_add(1, 1)
     line_edge(1, y2)
-    line_edge(0, y, first)
-    line_step(1, y1, 0)
-    line_step(0, y, 0, first)
+    ag_cross(0, 0)
     for s in range(2, nd):
         ag_cross(1, s)
     line_step(1, y2, 0)

time: 84 us -> 80.1 us (0.954)
  the two profiles are of different devices: /device:TPU:17 before, /device:TPU:21 now
where the time goes in v5:
time: 80.1 us; the launch traced here: 79.9 us
  Pallas kernels  66.3 us (83%)
  matrix products  12.3 us (15%)
    pallas_call x1, Pallas kernels, shards(): pl.pallas_call(functools.partial(exchange_kernel, rows, nd, cuts, tile),...  66.3 us
    dot_general x1, matrix products, shards(): lax.dot_general(feats.reshape(tokens, dm), grads.reshape(tokens, df), (((...  12.3 us

profile of v5, /device:TPU:21, one launch (start us, length us, event | category | flops | bytes accessed | tf_op | source)
XLA Modules:
  0.0 79.9 jit_solution(14004448412986032845)
XLA Ops:
  0.6 66.3 %exchange.1 = (f32[16,4096]{1,0:T(8,128)}, f32[16,16,4096]{2,1,0:T(8,128)}, f32[2,128,1024]{2,1,0:T(8,128)}) custom-call(f32[16,4096]{1,0:T(8,128)} %acts_ref.1, f32[128,1024]{1,0:T(8,128)} %grads_ref.1, f32[4096,1024]{1,0:T(8,128)} %weight_ref.1), custom_call_target="tpu_custom_call" | custom-call | flops 6442450944 | bytes 16777216 | tf_op jit(solution)/shard_map/exchange/pallas_call | solution.py:407
  66.9 0.0 copy-start
  66.9 12.3 %fusion = f32[4096,1024]{1,0:T(8,128)} fusion(f32[256,4096]{1,0:T(8,128)} %bitcast.4, f32[256,1024]{1,0:T(8,128)} %bitcast.5), kind=kOutput, calls=%fused_computation | convolution fusion | flops 6442450944 | bytes 22020096 | tf_op jit(solution)/shard_map/dot_general | solution.py:455
  79.2 0.0 copy-done
  79.2 0.7 copy.6
Async XLA Ops:
  66.9 12.3 %copy-start = (f32[16,4096]{1,0:T(8,128)S(1)}, f32[16,4096]{1,0:T(8,128)}, u32[]{:S(2)}) copy-start(f32[16,4096]{1,0:T(8,128)} %get-tuple-element.10) | copy-start | bytes 786436

commit v6 on v5

--- a/solution.py
+++ b/solution.py
@@ -399,7 +399,7 @@
     tokens = trow * rows
     tile = max(128, dm // 8)
     f32, bf16 = jnp.float32, jnp.bfloat16
-    cuts = (0, (dm // tile * 5 // 8) * tile, dm)
+    cuts = (0, (dm // tile * 4 // 8) * tile, dm)
     wa, wb = cuts[1], dm - cuts[1]
     vmem = pl.BlockSpec(memory_space=pltpu.VMEM)
     hbm = pl.BlockSpec(memory_space=pl.ANY)

time: 80.1 us -> 81.7 us (1.020)
  the two profiles are of different devices: /device:TPU:21 before, /device:TPU:13 now
where the time goes in v6:
time: 81.7 us; the launch traced here: 81.5 us
  Pallas kernels  67.9 us (83%)
  matrix products  12.3 us (15%)
    pallas_call x1, Pallas kernels, shards(): pl.pallas_call(functools.partial(exchange_kernel, rows, nd, cuts, tile),...  67.9 us
    dot_general x1, matrix products, shards(): lax.dot_general(feats.reshape(tokens, dm), grads.reshape(tokens, df), (((...  12.3 us

profile of v6, /device:TPU:13, one launch (start us, length us, event | category | flops | bytes accessed | tf_op | source)
XLA Modules:
  0.0 81.5 jit_solution(5304637215308756373)
XLA Ops:
  0.6 67.9 %exchange.1 = (f32[16,4096]{1,0:T(8,128)}, f32[16,16,4096]{2,1,0:T(8,128)}, f32[2,128,1024]{2,1,0:T(8,128)}) custom-call(f32[16,4096]{1,0:T(8,128)} %acts_ref.1, f32[128,1024]{1,0:T(8,128)} %grads_ref.1, f32[4096,1024]{1,0:T(8,128)} %weight_ref.1), custom_call_target="tpu_custom_call" | custom-call | flops 6442450944 | bytes 16777216 | tf_op jit(solution)/shard_map/exchange/pallas_call | solution.py:407
  68.5 0.0 copy-start
  68.5 12.3 %fusion = f32[4096,1024]{1,0:T(8,128)} fusion(f32[256,4096]{1,0:T(8,128)} %bitcast.4, f32[256,1024]{1,0:T(8,128)} %bitcast.5), kind=kOutput, calls=%fused_computation | convolution fusion | flops 6442450944 | bytes 22020096 | tf_op jit(solution)/shard_map/dot_general | solution.py:455
  80.8 0.0 copy-done
  80.8 0.7 copy.6
Async XLA Ops:
  68.5 12.3 %copy-start = (f32[16,4096]{1,0:T(8,128)S(1)}, f32[16,4096]{1,0:T(8,128)}, u32[]{:S(2)}) copy-start(f32[16,4096]{1,0:T(8,128)} %get-tuple-element.10) | copy-start | bytes 786436
